TPU v7x, 256 devices: a whole 4x4x8 slice. The times are simulated.
256 devices in a mesh: dp: 2 (over core), seq: 16 (over x_hi, z), chan: 8 (over y, x_lo).
Axes of the slice: x: 4 (x_hi: 2, x_lo: 2; x = x_hi * 2 + x_lo), y: 4, z: 8, core: 2. Of those that a mesh axis runs over, the one named last changes fastest.
Arguments:
- recurrence_feed: bfloat16 [8192, 8192], P(('dp', 'seq'), 'chan'), parts along dimension 0, may hold values from -6 to 6
- memory_write_matrix: bfloat16 [8192, 128], P(('dp', 'seq')), parts along dimension 0, may hold values from -0.5 to 0.5
- memory_read_matrix: bfloat16 [8192, 128], P(('dp', 'seq')), parts along dimension 0, may hold values from -0.5 to 0.5
- log_shrink_table: float32 [8192, 128], P(('dp', 'seq'), 'chan'), parts along dimension 0, may hold values from -0.5 to 0
- skip_connection_scale: float32 [128], P('chan'), may hold values from 0.5 to 2
- specialist_choices: int32 [8192, 2], P(('dp', 'seq')), parts along dimension 0, may hold values from 0 to 15, as said below
- specialist_mixing_shares: bfloat16 [8192, 2], P(('dp', 'seq')), parts along dimension 0, may hold values from 0.19921875 to 1
- specialist_rescale_vector: float32 [8192], P('chan'), may hold values from 0.25 to 1.75
- specialist_switch_matrix: bfloat16 [8192, 12288], P('chan', 'seq'), may hold values from -0.0625 to 0.0625
- specialist_widen_matrix: bfloat16 [8192, 12288], P('chan', 'seq'), may hold values from -0.0625 to 0.0625
- specialist_contract_matrix: bfloat16 [12288, 8192], P('seq', 'chan'), may hold values from -0.0546875 to 0.0546875
- closing_rescale_vector: float32 [8192], replicated, may hold values from 0.5 to 1.5
- lexicon_matrix: bfloat16 [8192, 32768], P(None, ('seq', 'chan')), may hold values from -19.887378 to 19.887378
- softness_divisor: float32 [1], replicated, may hold values from 0.5 to 1
- picked_entry_offsets: int32 [512], P(('dp', 'seq')), parts along dimension 0, may hold values from 0 to 255
Outputs:
- layer_out: bfloat16 [8192, 8192], P(('dp', 'seq'), 'chan'), parts along dimension 0
- log_probs: float32 [512, 32768], P('dp', ('seq', 'chan')), parts along dimension 0
There are 2 independent parts, one for each index of `dp`. A program takes and returns all parts, laid end to end along the dimension named above; an argument that names none is the same for every part. Nothing has to cross between parts.
Inputs may be any that keep to these rules, and one draw needn't show every extreme that they name: `specialist_choices`: the two experts of a row differ. In each aligned block of 256 rows, expert 0 is named by at most 64 rows, and by exactly 64 rows in some block.
All inputs are finite; a program needn't handle non-finite values.
Results may differ from a plain program's by a relative error of at most 0.01.
Values may be sent and summed in bfloat16 or wider, within the bound.
A program may use at most 64 MiB of HBM per device.

v0:
```python
import jax
import jax.numpy as jnp
from jax import lax
from jax.sharding import PartitionSpec as P

GROUP = 256


def carried_in(x, axis, combine, identity):
    devices, here = (lax.axis_size(axis), lax.axis_index(axis))
    everything = jax.tree.map(lambda part: lax.all_gather(part, axis), x)
    start = jax.tree.map(
        lambda part, zero: jnp.broadcast_to(jnp.asarray(zero, part.dtype), part.shape), x, identity
    )

    def hop(k, before):
        reached = k < here
        new = combine(before, jax.tree.map(lambda part: part[k], everything))
        return jax.tree.map(lambda a, b: jnp.where(reached, a, b), new, before)

    return lax.fori_loop(0, devices, hop, start)


def joined(part, axis, combine):
    gathered = jax.tree.map(lambda a: lax.all_gather(a, axis), part)

    def take(source):
        return jax.tree.map(lambda a: lax.dynamic_index_in_dim(a, source, 0, False), gathered)

    return lax.fori_loop(
        1, lax.axis_size(axis), lambda source, state: combine(state, take(source)), take(0)
    )


def compose(earlier, later):
    return (earlier[0] * later[0], later[0][:, None, None] * earlier[1] + later[1])


def combine_totals(first, second):
    top_value = jnp.maximum(first[0], second[0])
    return (
        top_value,
        first[1] * jnp.exp(first[0] - top_value) + second[1] * jnp.exp(second[0] - top_value),
    )


def shards(
    recurrence_feed,
    memory_write_matrix,
    memory_read_matrix,
    log_shrink_table,
    skip_connection_scale,
    specialist_choices,
    specialist_mixing_shares,
    specialist_rescale_vector,
    specialist_switch_matrix,
    specialist_widen_matrix,
    specialist_contract_matrix,
    closing_rescale_vector,
    lexicon_matrix,
    softness_divisor,
    picked_entry_offsets,
):
    shard_len, chan_width = recurrence_feed.shape
    head_count = log_shrink_table.shape[1]
    head_dim = chan_width // head_count
    state_dim = memory_write_matrix.shape[1]
    block_count = shard_len // GROUP
    chan_count = lax.axis_size("chan")
    capacity = shard_len // 4
    model_width = chan_width * chan_count
    x_blocks = recurrence_feed.reshape(block_count, GROUP, head_count, head_dim)
    b_blocks = memory_write_matrix.reshape(block_count, GROUP, state_dim)
    c_blocks = memory_read_matrix.reshape(block_count, GROUP, state_dim)
    cumulative = jnp.cumsum(log_shrink_table.reshape(block_count, GROUP, head_count), axis=1)
    scores = jnp.einsum("kin,kjn->kij", c_blocks, b_blocks, preferred_element_type=jnp.float32)
    causal = jnp.arange(GROUP)[:, None] >= jnp.arange(GROUP)[None, :]
    spread = cumulative[:, :, None, :] - cumulative[:, None, :, :]
    decay_mat = jnp.where(causal[None, :, :, None], jnp.exp(jnp.minimum(spread, 0.0)), 0.0)
    mixing = (scores[..., None] * decay_mat).astype(jnp.bfloat16)
    y_inner = jnp.einsum("kijh,kjhp->kihp", mixing, x_blocks, preferred_element_type=jnp.float32)
    tail_decay = jnp.exp(cumulative[:, -1:, :] - cumulative)
    weighted = (x_blocks.astype(jnp.float32) * tail_decay[..., None]).astype(jnp.bfloat16)
    local_state = jnp.einsum(
        "kjhp,kjn->khpn", weighted, b_blocks, preferred_element_type=jnp.float32
    )
    block_decay = jnp.exp(cumulative[:, -1, :])
    prefix_state = jnp.zeros((head_count, head_dim, state_dim), jnp.float32)
    prefix_decay = jnp.ones((head_count,), jnp.float32)
    prefix_list = prefix_state
    decay_list = prefix_decay
    prefix_state = block_decay[0][:, None, None] * prefix_state + local_state[0]
    prefix_decay = prefix_decay * block_decay[0]
    identity = (
        jnp.ones((head_count,), jnp.float32),
        jnp.zeros((head_count, head_dim, state_dim), jnp.float32),
    )
    entry_pair = carried_in((prefix_decay, prefix_state), "seq", compose, identity)
    entry_state = entry_pair[1]
    starts = jnp.stack([decay_list[:, None, None] * entry_state + prefix_list])
    y_outer = jnp.exp(cumulative)[..., None] * jnp.einsum(
        "kin,khpn->kihp", c_blocks.astype(jnp.float32), starts, precision=lax.Precision.HIGHEST
    )
    mamba_out = (
        y_inner
        + y_outer
        + skip_connection_scale[None, None, :, None] * x_blocks.astype(jnp.float32)
    )
    mamba_out = mamba_out.astype(jnp.bfloat16).reshape(shard_len, chan_width)
    chosen = specialist_choices == 0
    token_used = jnp.any(chosen, axis=1)
    gate_sum = jnp.sum(jnp.where(chosen, specialist_mixing_shares.astype(jnp.float32), 0.0), axis=1)
    place = jnp.cumsum(token_used.astype(jnp.int32)) - 1
    slot_map = (place[:, None] == jnp.arange(capacity, dtype=jnp.int32)[None, :]) & token_used[
        :, None
    ]
    slot_buffer = jnp.einsum(
        "tc,td->cd", slot_map.astype(jnp.bfloat16), mamba_out, preferred_element_type=jnp.float32
    ).astype(jnp.bfloat16)
    slot_rows = lax.all_gather(slot_buffer, "seq", axis=0, tiled=True)
    values = slot_rows.astype(jnp.float32)
    total_squares = lax.psum(jnp.sum(values * values, axis=-1), "chan")
    inv_rms = lax.rsqrt(total_squares / model_width + 1e-05)
    normed = (values * inv_rms[:, None] * specialist_rescale_vector).astype(jnp.bfloat16)
    gate_part = jnp.dot(normed, specialist_switch_matrix, preferred_element_type=jnp.float32)
    up_part = jnp.dot(normed, specialist_widen_matrix, preferred_element_type=jnp.float32)
    gate_total, up_total = (
        lax.psum(gate_part.astype(jnp.bfloat16), "chan").astype(jnp.float32),
        lax.psum(up_part.astype(jnp.bfloat16), "chan").astype(jnp.float32),
    )
    hidden = (jax.nn.silu(gate_total) * up_total).astype(jnp.bfloat16)
    expert_out = jnp.dot(hidden, specialist_contract_matrix, preferred_element_type=jnp.float32)
    returned = lax.psum_scatter(
        expert_out.astype(jnp.bfloat16), "seq", scatter_dimension=0, tiled=True
    ).astype(jnp.float32)
    slot_of_token = jnp.clip(place, 0, capacity - 1)
    contrib = jnp.take(returned, slot_of_token, axis=0)
    scale = jnp.where(token_used, gate_sum, 0.0)
    layer_out = (mamba_out.astype(jnp.float32) + scale[:, None] * contrib).astype(jnp.bfloat16)
    picked = jnp.take(layer_out, picked_entry_offsets, axis=0)
    full_rows = lax.all_gather(picked, "chan", axis=1, tiled=True).astype(jnp.float32)
    row_rms = lax.rsqrt(jnp.mean(full_rows * full_rows, axis=-1, keepdims=True) + 1e-05)
    normed_rows = (full_rows * row_rms * closing_rescale_vector).astype(jnp.bfloat16)
    lexicon_scores = jnp.dot(
        lax.all_gather(normed_rows, "seq", axis=0, tiled=True),
        lexicon_matrix,
        preferred_element_type=jnp.float32,
    )
    softened_scores = lexicon_scores / softness_divisor[0]
    row_peak = jnp.max(softened_scores, axis=1)
    row_mass = jnp.sum(jnp.exp(softened_scores - row_peak[:, None]), axis=1)
    global_peak, global_mass = joined((row_peak, row_mass), ("seq", "chan"), combine_totals)
    log_probs = softened_scores - global_peak[:, None] - jnp.log(global_mass)[:, None]
    return (layer_out, log_probs)


def solution(mesh):
    in_specs = (
        P(("dp", "seq"), "chan"),
        P(("dp", "seq"), None),
        P(("dp", "seq"), None),
        P(("dp", "seq"), "chan"),
        P("chan"),
        P(("dp", "seq"), None),
        P(("dp", "seq"), None),
        P("chan"),
        P("chan", "seq"),
        P("chan", "seq"),
        P("seq", "chan"),
        P(),
        P(None, ("seq", "chan")),
        P(),
        P(("dp", "seq")),
    )
    out_specs = (P(("dp", "seq"), "chan"), P("dp", ("seq", "chan")))
    return jax.shard_map(shards, mesh=mesh, in_specs=in_specs, out_specs=out_specs, check_vma=False)
```

profile of v0, /device:TPU:2, one launch (start us, length us, event | category | flops | bytes accessed | tf_op | source)
XLA Modules:
  0.0 1476.3 jit_solution(15853400060192934747)
XLA Ops:
  7.3 0.8 copy_bitcast_fusion.2
  8.1 0.6 reduce-window.15
  8.7 0.2 slice_reduce_fusion
  8.8 0.1 copy.52
  9.1 0.1 copy.58
  9.1 1.3 copy.55
  10.4 0.1 fusion.23
  10.5 1.1 convolution_add_fusion
  11.7 0.1 copy.56
  11.8 0.1 copy.53
  11.9 0.3 reduce-window.19
  12.2 0.1 slice.22
  12.3 42.7 %all-gather = f32[16,1,16]{2,1,0:T(1,128)S(1)} all-gather(f32[1,1,16]{2,1,0:T(1,128)S(1)} %get-tuple-element.296), channel_id=2, replica_groups=mesh['dp'=2,'seq'=16,'chan'=8] {'seq'}, dimensions={0}, use_global_device_ids=true | all-gather | bytes 1088 | tf_op jit(solution)/shard_map/all_gather | solution.py:11
  55.0 0.1 slice_reduce_fusion.1
  55.2 0.1 compare_and_fusion.1
  55.3 0.2 fusion.43
  55.5 94.0 %all-gather.14.cloned.1.call-done = f32[256,64,128]{2,1,0:T(8,128)} async-done(((f32[16,64,128]{2,1,0:T(8,128)}), f32[256,64,128]{2,1,0:T(8,128)}) %all-gather.14.cloned.1.call-update) | async-done | bytes 8388624 | tf_op jit(solution)/shard_map/all_gather | solution.py:11
  149.5 19.4 %while.32 = (s32[]{:T(128)}, f32[16,64,128]{2,1,0:T(8,128)S(1)}, s32[]{:T(128)}, f32[16,16]{1,0:T(8,128)S(1)}, f32[16,16,64,128]{3,2,1,0:T(8,128)}, /*index=5*/s32[]{:T(128)}, s32[]{:T(128)}) while((s32[]{:T(128)}, f32[16,64,128]{2,1,0:T(8,128)S(1)}, s32[]{:T(128)}, f32[16,16]{1,0:T(8,128)S(1)}, f32[16,16,64,128]{3,2,1,0:T(8,128)}, ...), condition=%wide.region_3.4_spmd.clone, body=%wide.region_2.3_spmd.clone.sunk | while | flops 524292 | bytes 1573161 | solution.py:21
  149.5 1.2 fusion.57
  150.7 1.2 fusion.57
  151.9 1.2 fusion.57
  153.1 1.2 fusion.57
  154.3 1.2 fusion.57
  155.6 1.2 fusion.57
  156.8 1.2 fusion.57
  158.0 1.2 fusion.57
  159.2 1.2 fusion.57
  160.4 1.2 fusion.57
  161.6 1.2 fusion.57
  162.8 1.2 fusion.57
  164.0 1.2 fusion.57
  165.3 1.2 fusion.57
  166.5 1.2 fusion.57
  167.7 1.2 fusion.57
  168.9 0.6 fusion.19
  169.5 1.5 fusion.22
  171.0 1.1 convolution_convert_fusion.3
  172.1 0.0 all-reduce.3.cloned.1.call-start
  172.2 82.4 %all-gather.10.cloned.1.call-done = bf16[1024,1024]{1,0:T(8,128)(2,1)} async-done(((bf16[64,1024]{1,0:T(8,128)(2,1)}), bf16[1024,1024]{1,0:T(8,128)(2,1)}) %all-gather.10.cloned.1.call-update) | async-done | bytes 2097168 | tf_op jit(solution)/shard_map/all_gather | solution.py:120
  254.6 2.1 fusion.1
  256.7 17.6 %psum.21 = f32[1024]{0:T(1024)S(1)} all-reduce(f32[1024]{0:T(1024)S(1)} %fusion.1), channel_id=1, replica_groups=mesh['dp'=2,'seq'=16,'chan'=8] {'chan'}, use_global_device_ids=true, to_apply=%region_9.10 | all-reduce | flops 1024 | bytes 8192 | tf_op jit(solution)/shard_map/psum | solution.py:122
  274.3 5.2 convolution_convert_fusion.2
  279.5 3.0 convolution_convert_fusion.1
  282.6 145.5 %all-reduce.3.cloned.1.call-done = (bf16[1024,768]{1,0:T(8,128)(2,1)}, bf16[1024,768]{1,0:T(8,128)(2,1)}) async-done(((bf16[1024,768]{1,0:T(8,128)(2,1)}, bf16[1024,768]{1,0:T(8,128)(2,1)}), (bf16[1024,768]{1,0:T(8,128)(2,1)}, bf16[1024,768]{1,0:T(8,128)(2,1)})) %all-reduce.3.cloned.1.call-update) | async-done | bytes 3145744 | tf_op jit(solution)/shard_map/psum | solution.py:129
  428.1 5.3 convolution_convert_fusion
  433.5 0.0 all-gather.12.cloned.1.call-start
  433.5 0.1 fusion.36
  433.7 0.2 copy.59
  433.9 207.5 %reduce-scatter.2.cloned.1.call-done = bf16[64,1024]{1,0:T(8,128)(2,1)} async-done(((bf16[1024,1024]{1,0:T(8,128)(2,1)}), bf16[64,1024]{1,0:T(8,128)(2,1)}) %reduce-scatter.2.cloned.1.call-update) | async-done | bytes 131088 | tf_op jit(solution)/shard_map/reduce_scatter | solution.py:133
  641.4 0.9 convert_element_type.112
  642.3 1.1 gather_fusion
  643.4 1.0 add_convert_fusion
  644.5 1.7 gather_fusion.1
  646.2 0.1 broadcast_select_fusion
  646.3 28.8 %all_gather.31 = bf16[16,8192]{1,0:T(8,128)(2,1)S(1)} all-gather(bf16[16,1024]{1,0:T(8,128)(2,1)S(1)} %broadcast_select_fusion), channel_id=1, replica_groups=mesh['dp'=2,'seq'=16,'chan'=8] {'chan'}, dimensions={1}, use_global_device_ids=true | all-gather | bytes 294912 | tf_op jit(solution)/shard_map/all_gather | solution.py:141
  675.1 0.2 fusion.26
  675.3 0.8 fusion.28
  676.8 97.2 %all-gather.12.cloned.1.call-done = bf16[256,8192]{1,0:T(8,128)(2,1)} async-done(((bf16[16,8192]{1,0:T(8,128)(2,1)}), bf16[256,8192]{1,0:T(8,128)(2,1)}) %all-gather.12.cloned.1.call-update) | async-done | bytes 4194320 | tf_op jit(solution)/shard_map/all_gather | solution.py:145
  773.9 5.2 fusion.42
  779.2 0.1 exponential_reduce_fusion
  779.2 339.4 %all-gather.5 = f32[128,1,256]{2,1,0:T(1,128)S(1)} all-gather(f32[1,1,256]{2,1,0:T(1,128)S(1)} %bitcast.129), channel_id=5, replica_groups=mesh['dp'=2,'seq'=16,'chan'=8] {'seq','chan'}, dimensions={0}, use_global_device_ids=true | all-gather | bytes 132096 | tf_op jit(solution)/shard_map/all_gather | solution.py:25
  1118.7 342.8 %all-gather.4 = f32[128,1,256]{2,1,0:T(1,128)S(1)} all-gather(f32[1,1,256]{2,1,0:T(1,128)S(1)} %bitcast.128), channel_id=4, replica_groups=mesh['dp'=2,'seq'=16,'chan'=8] {'seq','chan'}, dimensions={0}, use_global_device_ids=true | all-gather | bytes 132096 | tf_op jit(solution)/shard_map/all_gather | solution.py:25
  1461.5 7.4 while.31
  1468.9 0.8 copy.60
  (327 shorter events, 4.8 us)
Async XLA Ops:
  7.2 421.0 %copy-start = (bf16[768,1024]{1,0:T(8,128)(2,1)S(1)}, bf16[768,1024]{1,0:T(8,128)(2,1)}, u32[]{:S(2)}) copy-start(bf16[768,1024]{1,0:T(8,128)(2,1)} %param.29) | copy-start | bytes 4718596
  7.2 3.3 copy-start.2
  7.2 4.6 copy-start.5
  7.2 48.1 %copy-start.3 = (bf16[256,128]{1,0:T(8,128)(2,1)S(1)}, bf16[256,128]{1,0:T(8,128)(2,1)}, u32[]{:S(2)}) copy-start(bf16[256,128]{1,0:T(8,128)(2,1)} %param.21) | copy-start | bytes 196612
  7.2 142.3 %all-gather.14.cloned.1.call-start = ((), (), s32[]{:S(2)}) async-start(), calls=%async_computation.4 | async-start | bytes 8912896 | tf_op jit(solution)/shard_map/all_gather | solution.py:11
  11.6 243.0 %all-gather.10.cloned.1.call-start = ((), (), s32[]{:S(2)}) async-start(), calls=%async_computation.1 | async-start | bytes 2228224 | tf_op jit(solution)/shard_map/all_gather | solution.py:120
  149.5 20.0 %copy-start.9 = (f32[16]{0:T(128)S(1)}, f32[16]{0:T(128)}, u32[]{:S(2)}) copy-start(f32[16]{0:T(128)} %param.23) | copy-start | bytes 196
  169.5 104.8 %copy-start.8 = (f32[1024]{0:T(1024)S(1)}, f32[1024]{0:T(1024)}, u32[]{:S(2)}) copy-start(f32[1024]{0:T(1024)} %param.26) | copy-start | bytes 12292
  172.1 256.0 %all-reduce.3.cloned.1.call-start = ((), (), s32[]{:S(2)}) async-start(), calls=%async_computation.5 | async-start | bytes 6291456 | tf_op jit(solution)/shard_map/psum | solution.py:129
  274.2 5.3 copy-start.1
  274.3 5.3 copy-start.7
  282.6 358.8 %reduce-scatter.2.cloned.1.call-start = ((), (), s32[]{:S(2)}) async-start(), calls=%async_computation.2 | async-start | bytes 2228224 | tf_op jit(solution)/shard_map/reduce_scatter | solution.py:133
  428.1 5.5 copy-start.10
  428.1 5.5 copy-start.6
  433.5 340.5 %all-gather.12.cloned.1.call-start = ((), (), s32[]{:S(2)}) async-start(), calls=%async_computation.3 | async-start | bytes 4456448 | tf_op jit(solution)/shard_map/all_gather | solution.py:145
  642.3 32.9 %copy-start.4 = (f32[8192]{0:T(1024)S(1)}, f32[8192]{0:T(1024)}, u32[]{:S(2)}) copy-start(f32[8192]{0:T(1024)} %param.30) | copy-start | bytes 98308
Sparse Core Ops, SparseCore 0:
  11.7 137.6 all-gather.13
  172.2 82.3 all-gather.9
  282.7 145.4 all-reduce.2
  433.6 207.7 reduce-scatter.1
  676.3 97.6 all-gather.11
where the time goes:
time: 1480 us
  blocking collectives  771 us (52%)
  waiting for transfers between devices  627 us (42%)
  other arithmetic  28 us (2%)
  matrix products  23.2 us (2%)
    all_gather x2, blocking collectives, joined(): gathered = jax.tree.map(lambda a: lax.all_gather(a, axis), part)  682 us
    reduce_scatter x1, waiting for transfers between devices, shards(): lax.psum_scatter(expert_out.astype(jnp.bfloat16), 'seq', scatter_dimensio...  208 us
    psum x1, waiting for transfers between devices, shards(): lax.psum(up_part.astype(jnp.bfloat16), 'chan').astype(jnp.float32)  146 us
    all_gather x1, waiting for transfers between devices, shards(): lax.all_gather(normed_rows, 'seq', axis=0, tiled=True)  97.2 us
    all_gather x1, waiting for transfers between devices, carried_in(): everything = jax.tree.map(lambda part: lax.all_gather(part, axis), x)  94 us
    all_gather x1, waiting for transfers between devices, shards(): slot_rows = lax.all_gather(slot_buffer, 'seq', axis=0, tiled=True)  82.4 us
    all_gather x1, blocking collectives, carried_in(): everything = jax.tree.map(lambda part: lax.all_gather(part, axis), x)  42.7 us
  transfers between devices with their start and end apart: 5, of which 5 were waited for; matrix products, arithmetic and copies ran while one was open for 0% of the time, Pallas kernels for 0%

commit v1 on v0

--- a/solution.py
+++ b/solution.py
@@ -126,7 +126,7 @@
     up_part = jnp.dot(normed, specialist_widen_matrix, preferred_element_type=jnp.float32)
     gate_total, up_total = (
         lax.psum(gate_part.astype(jnp.bfloat16), "chan").astype(jnp.float32),
-        lax.psum(up_part.astype(jnp.bfloat16), "chan").astype(jnp.float32),
+        jnp.sum(lax.all_gather(up_part.astype(jnp.bfloat16), "chan"), axis=0).astype(jnp.float32),
     )
     hidden = (jax.nn.silu(gate_total) * up_total).astype(jnp.bfloat16)
     expert_out = jnp.dot(hidden, specialist_contract_matrix, preferred_element_type=jnp.float32)

time: 1480 us -> 1670 us (1.13)
  waiting for transfers between devices: 627 us -> 809 us
    all_gather x0 -> x1, waiting for transfers between devices: none -> 242 us  [shards(): lax.all_gather(up_part.astype(jnp.bfloat16), 'chan')]
    psum x1, waiting for transfers between devices: 146 us -> 86.9 us  [shards(): lax.psum(gate_part.astype(jnp.bfloat16), 'chan').astype(jnp.float32)]
  transfers between devices with their start and end apart: 5 -> 6, of which waited for: 5 -> 6; matrix products, arithmetic and copies ran while one was open for 0% -> 1% of each run, Pallas kernels for 0% -> 0%
where the time goes in v1:
time: 1670 us
  waiting for transfers between devices  809 us (48%)
  blocking collectives  772 us (46%)
  other arithmetic  35.9 us (2%)
  matrix products  25 us (1%)
    all_gather x2, blocking collectives, joined(): gathered = jax.tree.map(lambda a: lax.all_gather(a, axis), part)  682 us
    all_gather x1, waiting for transfers between devices, shards(): lax.all_gather(up_part.astype(jnp.bfloat16), 'chan')  242 us
    reduce_scatter x1, waiting for transfers between devices, shards(): lax.psum_scatter(expert_out.astype(jnp.bfloat16), 'seq', scatter_dimensio...  207 us
    all_gather x1, waiting for transfers between devices, shards(): lax.all_gather(normed_rows, 'seq', axis=0, tiled=True)  96.9 us
    all_gather x1, waiting for transfers between devices, carried_in(): everything = jax.tree.map(lambda part: lax.all_gather(part, axis), x)  94 us
    psum x1, waiting for transfers between devices, shards(): lax.psum(gate_part.astype(jnp.bfloat16), 'chan').astype(jnp.float32)  86.9 us
    all_gather x1, waiting for transfers between devices, shards(): slot_rows = lax.all_gather(slot_buffer, 'seq', axis=0, tiled=True)  82.4 us
    all_gather x1, blocking collectives, carried_in(): everything = jax.tree.map(lambda part: lax.all_gather(part, axis), x)  42.8 us
  transfers between devices with their start and end apart: 6, of which 6 were waited for; matrix products, arithmetic and copies ran while one was open for 1% of the time, Pallas kernels for 0%

profile of v1, /device:TPU:2, one launch (start us, length us, event | category | flops | bytes accessed | tf_op | source)
XLA Modules:
  0.0 1669.6 jit_solution(9380341796698615817)
XLA Ops:
  7.3 0.8 copy_bitcast_fusion.2
  8.1 0.6 reduce-window.15
  8.7 0.2 slice_reduce_fusion
  8.8 0.1 copy.52
  9.1 0.1 copy.58
  9.1 1.3 copy.55
  10.4 0.1 fusion.23
  10.5 1.1 convolution_add_fusion
  11.7 0.1 copy.56
  11.8 0.1 copy.53
  11.9 0.3 reduce-window.19
  12.2 0.1 slice.22
  12.3 42.8 %all-gather = f32[16,1,16]{2,1,0:T(1,128)S(1)} all-gather(f32[1,1,16]{2,1,0:T(1,128)S(1)} %get-tuple-element.294), channel_id=2, replica_groups=mesh['dp'=2,'seq'=16,'chan'=8] {'seq'}, dimensions={0}, use_global_device_ids=true | all-gather | bytes 1088 | tf_op jit(solution)/shard_map/all_gather | solution.py:11
  55.0 0.1 slice_reduce_fusion.1
  55.2 0.1 compare_and_fusion.1
  55.3 0.2 fusion.43
  55.5 94.0 %all-gather.16.cloned.1.call-done = f32[256,64,128]{2,1,0:T(8,128)} async-done(((f32[16,64,128]{2,1,0:T(8,128)}), f32[256,64,128]{2,1,0:T(8,128)}) %all-gather.16.cloned.1.call-update) | async-done | bytes 8388624 | tf_op jit(solution)/shard_map/all_gather | solution.py:11
  149.5 19.4 %while.32 = (s32[]{:T(128)}, f32[16,64,128]{2,1,0:T(8,128)S(1)}, s32[]{:T(128)}, f32[16,16]{1,0:T(8,128)S(1)}, f32[16,16,64,128]{3,2,1,0:T(8,128)}, /*index=5*/s32[]{:T(128)}, s32[]{:T(128)}) while((s32[]{:T(128)}, f32[16,64,128]{2,1,0:T(8,128)S(1)}, s32[]{:T(128)}, f32[16,16]{1,0:T(8,128)S(1)}, f32[16,16,64,128]{3,2,1,0:T(8,128)}, ...), condition=%wide.region_3.4_spmd.clone, body=%wide.region_2.3_spmd.clone.sunk | while | flops 524292 | bytes 1573161 | solution.py:21
  149.5 1.2 fusion.57
  150.7 1.2 fusion.57
  151.9 1.2 fusion.57
  153.1 1.2 fusion.57
  154.3 1.2 fusion.57
  155.5 1.2 fusion.57
  156.8 1.2 fusion.57
  158.0 1.2 fusion.57
  159.2 1.2 fusion.57
  160.4 1.2 fusion.57
  161.6 1.2 fusion.57
  162.8 1.2 fusion.57
  164.0 1.2 fusion.57
  165.3 1.2 fusion.57
  166.5 1.2 fusion.57
  167.7 1.2 fusion.57
  168.9 0.6 fusion.19
  169.5 1.5 fusion.22
  171.0 1.1 convolution_convert_fusion.3
  172.2 82.4 %all-gather.12.cloned.1.call-done = bf16[1024,1024]{1,0:T(8,128)(2,1)} async-done(((bf16[64,1024]{1,0:T(8,128)(2,1)}), bf16[1024,1024]{1,0:T(8,128)(2,1)}) %all-gather.12.cloned.1.call-update) | async-done | bytes 2097168 | tf_op jit(solution)/shard_map/all_gather | solution.py:120
  254.6 2.1 fusion.1
  256.7 17.6 %psum.14 = f32[1024]{0:T(1024)S(1)} all-reduce(f32[1024]{0:T(1024)S(1)} %fusion.1), channel_id=1, replica_groups=mesh['dp'=2,'seq'=16,'chan'=8] {'chan'}, use_global_device_ids=true, to_apply=%region_9.10 | all-reduce | flops 1024 | bytes 8192 | tf_op jit(solution)/shard_map/psum | solution.py:122
  274.2 5.0 convolution_convert_fusion.1
  279.4 5.1 convolution_convert_fusion.2
  284.5 241.7 %all-gather.18.cloned.1.call-done = bf16[8192,768]{1,0:T(8,128)(2,1)} async-done(((bf16[1024,768]{1,0:T(8,128)(2,1)}), bf16[8192,768]{1,0:T(8,128)(2,1)}) %all-gather.18.cloned.1.call-update) | async-done | bytes 12582928 | tf_op jit(solution)/shard_map/all_gather | solution.py:129
  526.2 7.9 reduce_sum.50
  534.1 86.9 %all-reduce.2.cloned.1.call-done = bf16[1024,768]{1,0:T(8,128)(2,1)} async-done(((bf16[1024,768]{1,0:T(8,128)(2,1)}), bf16[1024,768]{1,0:T(8,128)(2,1)}) %all-reduce.2.cloned.1.call-update) | async-done | bytes 1572880 | tf_op jit(solution)/shard_map/psum | solution.py:128
  621.0 5.3 convolution_convert_fusion
  626.3 0.1 fusion.36
  626.5 0.2 copy.59
  626.7 207.3 %reduce-scatter.2.cloned.1.call-done = bf16[64,1024]{1,0:T(8,128)(2,1)} async-done(((bf16[1024,1024]{1,0:T(8,128)(2,1)}), bf16[64,1024]{1,0:T(8,128)(2,1)}) %reduce-scatter.2.cloned.1.call-update) | async-done | bytes 131088 | tf_op jit(solution)/shard_map/reduce_scatter | solution.py:133
  834.0 0.9 convert_element_type.114
  835.0 1.1 gather_fusion
  836.1 1.0 add_convert_fusion
  837.1 1.7 gather_fusion.1
  838.8 0.1 broadcast_select_fusion
  838.9 29.4 %all_gather.39 = bf16[16,8192]{1,0:T(8,128)(2,1)S(1)} all-gather(bf16[16,1024]{1,0:T(8,128)(2,1)S(1)} %broadcast_select_fusion), channel_id=1, replica_groups=mesh['dp'=2,'seq'=16,'chan'=8] {'chan'}, dimensions={1}, use_global_device_ids=true | all-gather | bytes 294912 | tf_op jit(solution)/shard_map/all_gather | solution.py:141
  868.3 0.2 fusion.26
  868.5 0.8 fusion.28
  870.0 96.9 %all-gather.14.cloned.1.call-done = bf16[256,8192]{1,0:T(8,128)(2,1)} async-done(((bf16[16,8192]{1,0:T(8,128)(2,1)}), bf16[256,8192]{1,0:T(8,128)(2,1)}) %all-gather.14.cloned.1.call-update) | async-done | bytes 4194320 | tf_op jit(solution)/shard_map/all_gather | solution.py:145
  966.9 5.2 fusion.42
  972.1 0.1 exponential_reduce_fusion
  972.2 339.4 %all-gather.6 = f32[128,1,256]{2,1,0:T(1,128)S(1)} all-gather(f32[1,1,256]{2,1,0:T(1,128)S(1)} %bitcast.131), channel_id=6, replica_groups=mesh['dp'=2,'seq'=16,'chan'=8] {'seq','chan'}, dimensions={0}, use_global_device_ids=true | all-gather | bytes 132096 | tf_op jit(solution)/shard_map/all_gather | solution.py:25
  1311.7 342.8 %all-gather.5 = f32[128,1,256]{2,1,0:T(1,128)S(1)} all-gather(f32[1,1,256]{2,1,0:T(1,128)S(1)} %bitcast.130), channel_id=5, replica_groups=mesh['dp'=2,'seq'=16,'chan'=8] {'seq','chan'}, dimensions={0}, use_global_device_ids=true | all-gather | bytes 132096 | tf_op jit(solution)/shard_map/all_gather | solution.py:25
  1654.5 7.4 while.31
  1661.9 0.8 copy.60
  (327 shorter events, 4.9 us)
Async XLA Ops:
  7.2 613.8 %copy-start = (bf16[768,1024]{1,0:T(8,128)(2,1)S(1)}, bf16[768,1024]{1,0:T(8,128)(2,1)}, u32[]{:S(2)}) copy-start(bf16[768,1024]{1,0:T(8,128)(2,1)} %param.29) | copy-start | bytes 4718596
  7.2 3.3 copy-start.1
  7.2 4.6 copy-start.4
  7.2 48.1 %copy-start.2 = (bf16[256,128]{1,0:T(8,128)(2,1)S(1)}, bf16[256,128]{1,0:T(8,128)(2,1)}, u32[]{:S(2)}) copy-start(bf16[256,128]{1,0:T(8,128)(2,1)} %param.21) | copy-start | bytes 196612
  7.2 142.2 %all-gather.16.cloned.1.call-start = ((), (), s32[]{:S(2)}) async-start(), calls=%async_computation.5 | async-start | bytes 8912896 | tf_op jit(solution)/shard_map/all_gather | solution.py:11
  11.6 243.0 %all-gather.12.cloned.1.call-start = ((), (), s32[]{:S(2)}) async-start(), calls=%async_computation.1 | async-start | bytes 2228224 | tf_op jit(solution)/shard_map/all_gather | solution.py:120
  149.5 20.0 %copy-start.7 = (f32[16]{0:T(128)S(1)}, f32[16]{0:T(128)}, u32[]{:S(2)}) copy-start(f32[16]{0:T(128)} %param.23) | copy-start | bytes 196
  169.5 104.8 %copy-start.6 = (f32[1024]{0:T(1024)S(1)}, f32[1024]{0:T(1024)}, u32[]{:S(2)}) copy-start(f32[1024]{0:T(1024)} %param.26) | copy-start | bytes 12292
  172.1 354.1 %all-gather.18.cloned.1.call-start = ((), (), s32[]{:S(2)}) async-start(), calls=%async_computation.6 | async-start | bytes 14155776 | tf_op jit(solution)/shard_map/all_gather | solution.py:129
  279.3 341.7 %all-reduce.2.cloned.1.call-start = ((), (), s32[]{:S(2)}) async-start(), calls=%async_computation.2 | async-start | bytes 3145728 | tf_op jit(solution)/shard_map/psum | solution.py:128
  284.4 549.6 %reduce-scatter.2.cloned.1.call-start = ((), (), s32[]{:S(2)}) async-start(), calls=%async_computation.3 | async-start | bytes 2228224 | tf_op jit(solution)/shard_map/reduce_scatter | solution.py:133
  534.1 92.3 %copy-start.8 = (s32[16]{0:T(128)S(1)}, s32[16]{0:T(128)}, u32[]{:S(2)}) copy-start(s32[16]{0:T(128)} %param.33) | copy-start | bytes 196
  534.1 92.3 %copy-start.5 = (bf16[256,2]{0,1:T(2,128)(2,1)S(1)}, bf16[256,2]{0,1:T(2,128)(2,1)}, u32[]{:S(2)}) copy-start(bf16[256,2]{0,1:T(2,128)(2,1)} %param.25) | copy-start | bytes 3076
  626.3 340.6 %all-gather.14.cloned.1.call-start = ((), (), s32[]{:S(2)}) async-start(), calls=%async_computation.4 | async-start | bytes 4456448 | tf_op jit(solution)/shard_map/all_gather | solution.py:145
  835.0 33.5 %copy-start.3 = (f32[8192]{0:T(1024)S(1)}, f32[8192]{0:T(1024)}, u32[]{:S(2)}) copy-start(f32[8192]{0:T(1024)} %param.30) | copy-start | bytes 98308
Sparse Core Ops, SparseCore 0:
  11.8 137.6 all-gather.15
  172.2 82.3 all-gather.11
  279.4 246.7 all-gather.17
  528.8 92.1 all-reduce.1
  626.4 207.5 reduce-scatter.1
  869.5 97.3 all-gather.13
